TPU v7x, 32 devices: a whole 2x2x4 slice. The times are simulated.
32 devices in a mesh: groups: 2 (over x), seq: 16 (over z, y, core).
Axes of the slice: x: 2, y: 2, z: 4, core: 2. Of those that a mesh axis runs over, the one named last changes fastest.
Arguments:
- queries: bfloat16 [32, 4, 8192], P(('groups', 'seq')), parts along dimension 0, may hold values from -256 to 256
- base_cache: bfloat16 [16384, 2048], P(('groups', 'seq')), parts along dimension 0, may hold values from -8 to 8
- page_pool: bfloat16 [64, 128, 2048], P(('groups', 'seq')), parts along dimension 0, may hold values from -6 to 6
- new_cache: bfloat16 [32, 4, 2048], P(('groups', 'seq')), parts along dimension 0, may hold values from -12 to 12
- page_table: int32 [32, 2], P('groups'), parts along dimension 0, may hold values from 0 to 31, as said below
- offsets: int32 [32], P('groups'), parts along dimension 0, may hold values from 1024 to 8192
- lengths: int32 [32], P('groups'), parts along dimension 0, may hold values from 1 to 256
Outputs:
- attended: bfloat16 [32, 4, 8192], P(('groups', 'seq')), parts along dimension 0
There are 2 independent parts, one for each index of `groups`. A program takes and returns all parts, laid end to end along the dimension named above; each array names one. Nothing has to cross between parts.
Inputs may be any that keep to these rules, and one draw needn't show every extreme that they name: `page_table`: each of the 32 pool pages is named by exactly one entry.
All inputs are finite; a program needn't handle non-finite values.
Results may differ from a plain program's by a relative error of at most 0.0075.
Values may be sent and summed in bfloat16 or wider, within the bound.
A program may use at most 128 MiB of HBM per device.

v0:
```python
import jax
import jax.numpy as jnp
from jax import lax
from jax.sharding import PartitionSpec as P

QH = 64
KVH = 8
HD = 128


far_below = -1e30
strict_setting = lax.Precision.HIGHEST


def head_column_span(source, head_id, offset):
    start = head_id * 2 * HD + offset
    return source[..., start : start + HD]


def score_blocks(gathered, base_cache, page_pool, page_queries, head_id, base_live, page_live):
    overall_rows, step_count, full_width = gathered.shape
    pool_count = page_pool.shape[0]
    group_size = QH // KVH
    score_scale = HD ** (-0.5)
    first_col = head_id * group_size * HD
    last_col = first_col + group_size * HD
    row_queries = gathered[:, :, first_col:last_col].reshape(
        overall_rows, step_count * group_size, HD
    )
    base_scores = (
        jnp.einsum(
            "rux,zx->ruz",
            row_queries,
            head_column_span(base_cache, head_id, 0),
            preferred_element_type=jnp.float32,
        )
        * score_scale
    )
    base_scores = jnp.where(base_live[:, None, :], base_scores, far_below)
    pool_queries = page_queries[:, :, first_col:last_col].reshape(
        pool_count, step_count * group_size, HD
    )
    page_scores = (
        jnp.einsum(
            "pqd,pkd->pqk",
            pool_queries,
            head_column_span(page_pool, head_id, 0),
            preferred_element_type=jnp.float32,
        )
        * score_scale
    )
    page_scores = jnp.where(page_live[:, None, :], page_scores, far_below)
    return (base_scores, page_scores)


def local_maximum(base_scores, page_scores, row_match):
    page_best = jnp.max(page_scores, axis=2)
    spread = jnp.where(row_match[:, :, None], page_best[None, :, :], far_below)
    return jnp.maximum(jnp.max(base_scores, axis=2), jnp.max(spread, axis=1))


def accumulate(
    gathered,
    base_cache,
    page_pool,
    page_queries,
    base_live,
    page_live,
    row_match,
    owner_row,
    given_top,
):
    overall_rows, step_count, full_width = gathered.shape
    group_size = QH // KVH
    row_selection = row_match.astype(jnp.float32)
    numer_heads = []
    denom_heads = []
    top_heads = []
    for head_id in range(KVH):
        base_scores, page_scores = score_blocks(
            gathered, base_cache, page_pool, page_queries, head_id, base_live, page_live
        )
        row_top = given_top[:, :, head_id * group_size : (head_id + 1) * group_size].reshape(
            overall_rows, step_count * group_size
        )
        page_top = row_top[owner_row]
        prefix_weights = jnp.where(
            base_live[:, None, :], jnp.exp(base_scores - row_top[:, :, None]), 0.0
        )
        page_weights = jnp.where(
            page_live[:, None, :], jnp.exp(page_scores - page_top[:, :, None]), 0.0
        )
        numerator = jnp.einsum(
            "lip,pn->lin",
            prefix_weights.astype(jnp.bfloat16),
            head_column_span(base_cache, head_id, HD),
            preferred_element_type=jnp.float32,
        )
        page_contributions = jnp.einsum(
            "pqk,pkd->pqd",
            page_weights.astype(jnp.bfloat16),
            head_column_span(page_pool, head_id, HD),
            preferred_element_type=jnp.float32,
        )
        numerator = numerator + jnp.einsum(
            "zv,vsx->zsx", row_selection, page_contributions, precision=strict_setting
        )
        denominator = jnp.sum(prefix_weights, axis=2) + jnp.dot(
            row_selection, jnp.sum(page_weights, axis=2), precision=strict_setting
        )
        numer_heads.append(numerator.reshape(overall_rows, step_count, group_size * HD))
        denom_heads.append(denominator.reshape(overall_rows, step_count, group_size))
        top_heads.append(row_top.reshape(overall_rows, step_count, group_size))
    return (
        jnp.concatenate(numer_heads, axis=2),
        jnp.concatenate(denom_heads, axis=2),
        jnp.concatenate(top_heads, axis=2),
    )


def settle(num_parts, den_parts, top_parts, queries, new_cache):
    source_count, rows_here, step_count, full_width = num_parts.shape
    group_size = QH // KVH
    score_scale = HD ** (-0.5)
    own_queries = queries.reshape(rows_here, step_count, KVH, group_size, HD)
    fresh_cache = new_cache.reshape(rows_here, step_count, KVH, 2, HD)
    new_scores = (
        jnp.einsum(
            "rshgd,ruhd->rshgu",
            own_queries,
            fresh_cache[:, :, :, 0, :],
            preferred_element_type=jnp.float32,
        )
        * score_scale
    )
    step_ids = jnp.arange(step_count, dtype=jnp.int32)
    causal = (step_ids[None, :] <= step_ids[:, None])[None, :, None, None, :]
    new_scores = jnp.where(causal, new_scores, far_below)
    new_top = jnp.max(new_scores, axis=4).reshape(rows_here, step_count, QH)
    row_top = jnp.maximum(jnp.max(top_parts, axis=0), new_top)
    factor = jnp.exp(top_parts - row_top[None])
    numerator = jnp.sum(
        num_parts.reshape(source_count, rows_here, step_count, QH, HD) * factor[..., None], axis=0
    )
    denominator = jnp.sum(den_parts * factor, axis=0)
    top_split = row_top.reshape(rows_here, step_count, KVH, group_size)
    new_weights = jnp.where(causal, jnp.exp(new_scores - top_split[..., None]), 0.0)
    new_terms = jnp.einsum(
        "rshgu,ruhd->rshgd",
        new_weights.astype(jnp.bfloat16),
        fresh_cache[:, :, :, 1, :],
        preferred_element_type=jnp.float32,
    )
    numerator = numerator + new_terms.reshape(rows_here, step_count, QH, HD)
    denominator = denominator + jnp.sum(new_weights, axis=4).reshape(rows_here, step_count, QH)
    return (
        (numerator / denominator[..., None])
        .reshape(rows_here, step_count, QH * HD)
        .astype(jnp.bfloat16)
    )


def page_setup(gathered, page_table, lengths, offsets, base_length, pool_count, page_length):
    device = lax.axis_index("seq")
    overall_rows, page_slots = page_table.shape
    base_place = device * base_length + jnp.arange(base_length, dtype=jnp.int32)
    base_live = base_place[None, :] < offsets[:, None]
    page_ids = device * pool_count + jnp.arange(pool_count, dtype=jnp.int32)
    flat_table = page_table.reshape(-1)
    page_match = flat_table[None, :] == page_ids[:, None]
    entry_ids = jnp.arange(overall_rows * page_slots, dtype=jnp.int32)
    table_entry = jnp.sum(jnp.where(page_match, entry_ids[None, :], 0), axis=1)
    owner_row = table_entry // page_slots
    owner_page = table_entry % page_slots
    page_queries = gathered[owner_row]
    page_place = (
        owner_page[:, None] * page_length + jnp.arange(page_length, dtype=jnp.int32)[None, :]
    )
    page_live = page_place < lengths[owner_row][:, None]
    row_match = jnp.arange(overall_rows, dtype=jnp.int32)[:, None] == owner_row[None, :]
    return (base_live, owner_row, page_queries, page_live, row_match)


def body(queries, base_cache, page_pool, new_cache, page_table, offsets, lengths):
    device = lax.axis_index("seq")
    rows_here, step_count, full_width = queries.shape
    overall_rows, page_slots = page_table.shape
    base_length = base_cache.shape[0]
    pool_count = page_pool.shape[0]
    page_length = page_pool.shape[1]
    gathered = lax.all_gather(queries, "seq", axis=0, tiled=True)
    base_live, owner_row, page_queries, page_live, row_match = page_setup(
        gathered, page_table, lengths, offsets, base_length, pool_count, page_length
    )
    group_size = QH // KVH
    head_tops = []
    for head_id in range(KVH):
        base_scores, page_scores = score_blocks(
            gathered, base_cache, page_pool, page_queries, head_id, base_live, page_live
        )
        head_tops.append(
            local_maximum(base_scores, page_scores, row_match).reshape(
                overall_rows, step_count, group_size
            )
        )
    nearby_maximum = jnp.concatenate(head_tops, axis=2)
    global_top = lax.pmax(nearby_maximum.astype(jnp.bfloat16), "seq").astype(nearby_maximum.dtype)
    numerator, denominator, unused_top = accumulate(
        gathered,
        base_cache,
        page_pool,
        page_queries,
        base_live,
        page_live,
        row_match,
        owner_row,
        global_top,
    )
    numerator, denominator = (
        lax.psum_scatter(numerator, "seq", scatter_dimension=0, tiled=True),
        lax.psum_scatter(denominator, "seq", scatter_dimension=0, tiled=True),
    )
    own_top = lax.dynamic_slice_in_dim(global_top, device * rows_here, rows_here, 0)
    return settle(numerator[None], denominator[None], own_top[None], queries, new_cache)


def solution(mesh):
    in_specs = (
        P(("groups", "seq"), None, None),
        P(("groups", "seq"), None),
        P(("groups", "seq"), None, None),
        P(("groups", "seq"), None, None),
        P("groups", None),
        P("groups"),
        P("groups"),
    )
    out_specs = P(("groups", "seq"), None, None)
    return jax.shard_map(body, mesh=mesh, in_specs=in_specs, out_specs=out_specs, check_vma=False)
```

profile of v0, /device:TPU:0, one launch (start us, length us, event | category | flops | bytes accessed | tf_op | source)
XLA Modules:
  0.0 347.4 jit_solution(7498543012359663722)
XLA Ops:
  8.7 1.9 fusion.250
  12.8 1.3 dynamic-slice
  15.9 34.3 %all-gather.2.cloned.1.call-done = bf16[16,4,8192]{2,1,0:T(4,128)(2,1)} async-done(((bf16[1,4,8192]{2,1,0:T(4,128)(2,1)}), bf16[16,4,8192]{2,1,0:T(4,128)(2,1)}) %all-gather.2.cloned.1.call-update) | async-done | bytes 1048592 | tf_op jit(solution)/shard_map/all_gather | solution.py:191
  50.2 1.7 fusion.246
  52.0 1.9 gather_fusion.1
  63.8 1.3 fusion.260
  65.3 1.4 fusion.261
  68.0 1.3 copy.279
  69.3 1.4 copy.287
  70.7 2.3 fusion.262
  74.2 1.3 copy.280
  75.6 1.4 copy.288
  76.9 2.3 fusion.263
  80.5 1.4 copy.281
  81.9 1.4 copy.289
  83.3 2.3 fusion.264
  86.8 1.3 copy.282
  88.1 1.4 copy.290
  89.5 2.2 fusion.265
  91.7 1.3 max.121
  93.0 1.4 copy.283
  94.4 1.4 copy.291
  95.8 2.2 fusion.266
  99.9 59.7 %pmax.7 = bf16[16,4,64]{2,1,0:T(4,128)(2,1)S(1)} all-reduce(bf16[16,4,64]{2,1,0:T(4,128)(2,1)S(1)} %concatenate.10), channel_id=1, replica_groups=mesh['groups'=2,'seq'=16] {'seq'}, use_global_device_ids=true, to_apply=%region_25.26 | all-reduce | flops 4096 | bytes 16384 | tf_op jit(solution)/shard_map/pmax | solution.py:207
  176.0 1.7 fusion.116
  177.7 1.7 fusion.114
  179.3 1.6 fusion.112
  181.0 1.6 fusion.110
  182.6 1.6 fusion.108
  184.3 1.6 fusion.106
  185.9 1.6 fusion.104
  187.6 1.7 fusion.163
  196.0 4.1 %fusion.32 = (f32[16,32]{1,0:T(8,128)S(1)}, f32[16,32]{1,0:T(8,128)S(1)}, f32[16,32]{1,0:T(8,128)S(1)}, f32[16,32]{1,0:T(8,128)S(1)}, f32[16,32]{1,0:T(8,128)S(1...) fusion(f32[16,32,512]{2,1,0:T(8,128)} %get-tuple-element.92, f32[16,32]{1,0:T(8,128)S(1)} %copy.329, ...), kind=kLoop, calls=%fused_computation.84 | loop fusion | flops 6287360 | bytes 8429568 | tf_op jit(solution)/shard_map/reduce_sum | solution.py:108
  207.1 2.3 convolution_add_fusion
  210.9 2.3 convolution_add_fusion.1
  213.2 1.8 reshape.510
  215.4 2.3 convolution_add_fusion.2
  217.7 1.8 reshape.509
  220.0 2.3 convolution_add_fusion.3
  222.3 1.7 reshape.508
  224.5 2.3 convolution_add_fusion.4
  226.8 1.7 reshape.507
  229.0 2.0 convolution_add_fusion.5
  230.9 1.8 reshape.506
  235.6 1.3 convolution_add_fusion.7
  242.6 57.9 %all-reduce.1 = f32[16,4,64]{2,1,0:T(4,128)S(1)} all-reduce(f32[16,4,64]{2,1,0:T(4,128)S(1)} %copy.348), channel_id=3, replica_groups=mesh['groups'=2,'seq'=16] {'seq'}, use_global_device_ids=true, to_apply=%region_44.45.clone | all-reduce | flops 4096 | bytes 32768
  301.2 36.5 %all-reduce.4.cloned.1.call-done = f32[16,4,8192]{2,1,0:T(4,128)} async-done(((f32[16,4,8192]{2,1,0:T(4,128)}), f32[16,4,8192]{2,1,0:T(4,128)}) %all-reduce.4.cloned.1.call-update) | async-done | bytes 2097168
  337.7 1.6 constant_dynamic-slice_fusion
  (258 shorter events, 66.6 us)
Async XLA Ops:
  6.5 7.8 %copy-start = (s32[16]{0:T(128)S(1)}, s32[16]{0:T(128)}, u32[]{:S(2)}) copy-start(s32[16]{0:T(128)} %param.13) | copy-start | bytes 196
  6.5 43.7 %all-gather.2.cloned.1.call-start = ((), (), s32[]{:S(2)}) async-start(), calls=%async_computation | async-start | bytes 1114112 | tf_op jit(solution)/shard_map/all_gather | solution.py:191
  7.3 330.4 %all-reduce.4.cloned.1.call-start = ((), (), s32[]{:S(2)}) async-start(), calls=%async_computation.1 | async-start | bytes 4194304
  8.0 46.1 %copy-start.2 = (bf16[2,128,2048]{2,1,0:T(8,128)(2,1)S(1)}, bf16[2,128,2048]{2,1,0:T(8,128)(2,1)}, u32[]{:S(2)}) copy-start(bf16[2,128,2048]{2,1,0:T(8,128)(2,1)} %param.9) | copy-start | bytes 3145732
  8.7 1.9 copy-start.46
  10.6 5.3 %copy-start.31 = (f32[4,8,8]{2,0,1:T(4,128)}, f32[4,8,8]{2,0,1:T(4,128)S(1)}, u32[]{:S(2)}) copy-start(f32[4,8,8]{2,0,1:T(4,128)S(1)} %get-tuple-element.59) | copy-start | bytes 3076
  14.3 39.6 %copy-start.40 = (s32[1024]{0:T(1024)}, s32[1024]{0:T(1024)S(1)}, u32[]{:S(2)}) copy-start(s32[1024]{0:T(1024)S(1)} %pad_clamp_fusion) | copy-start | bytes 12292
  91.7 89.3 %copy-start.8 = (f32[2,32,128]{2,1,0:T(8,128)S(1)}, f32[2,32,128]{2,1,0:T(8,128)}, u32[]{:S(2)}) copy-start(f32[2,32,128]{2,1,0:T(8,128)} %get-tuple-element.66) | copy-start | bytes 98308
  91.7 90.9 %copy-start.9 = (f32[2,32,128]{2,1,0:T(8,128)S(1)}, f32[2,32,128]{2,1,0:T(8,128)}, u32[]{:S(2)}) copy-start(f32[2,32,128]{2,1,0:T(8,128)} %get-tuple-element.68) | copy-start | bytes 98308
  91.7 92.5 %copy-start.10 = (f32[2,32,128]{2,1,0:T(8,128)S(1)}, f32[2,32,128]{2,1,0:T(8,128)}, u32[]{:S(2)}) copy-start(f32[2,32,128]{2,1,0:T(8,128)} %get-tuple-element.70) | copy-start | bytes 98308
  91.7 94.2 %copy-start.11 = (f32[2,32,128]{2,1,0:T(8,128)S(1)}, f32[2,32,128]{2,1,0:T(8,128)}, u32[]{:S(2)}) copy-start(f32[2,32,128]{2,1,0:T(8,128)} %get-tuple-element.72) | copy-start | bytes 98308
  97.9 95.0 %copy-start.12 = (f32[1,4,8,8,4]{3,4,1,2,0:T(4,128)S(1)}, f32[1,4,8,8,4]{3,4,1,2,0:T(4,128)}, u32[]{:S(2)}) copy-start(f32[1,4,8,8,4]{3,4,1,2,0:T(4,128)} %get-tuple-element.60) | copy-start | bytes 12292
  161.0 33.4 %copy-start.37 = (bf16[1,4,8,1,128]{4,3,2,1,0:T(2,128)(2,1)S(1)}, bf16[1,4,8,1,128]{4,3,2,1,0:T(2,128)(2,1)}, u32[]{:S(2)}) copy-start(bf16[1,4,8,1,128]{4,3,2,1,0:T(2,128)(2,1)} %get-tuple-element.47) | copy-start | bytes 24580
  161.1 39.1 %copy-start.22 = (f32[16,32]{1,0:T(8,128)}, f32[16,32]{1,0:T(8,128)S(1)}, u32[]{:S(2)}) copy-start(f32[16,32]{1,0:T(8,128)S(1)} %copy.324) | copy-start | bytes 6148
  162.5 37.7 %copy-start.20 = (f32[16,32]{1,0:T(8,128)}, f32[16,32]{1,0:T(8,128)S(1)}, u32[]{:S(2)}) copy-start(f32[16,32]{1,0:T(8,128)S(1)} %copy.319) | copy-start | bytes 6148
  164.6 35.6 %copy-start.18 = (f32[16,32]{1,0:T(8,128)}, f32[16,32]{1,0:T(8,128)S(1)}, u32[]{:S(2)}) copy-start(f32[16,32]{1,0:T(8,128)S(1)} %copy.314) | copy-start | bytes 6148
  166.8 33.5 %copy-start.16 = (f32[16,32]{1,0:T(8,128)}, f32[16,32]{1,0:T(8,128)S(1)}, u32[]{:S(2)}) copy-start(f32[16,32]{1,0:T(8,128)S(1)} %copy.309) | copy-start | bytes 6148
  168.9 31.4 %copy-start.14 = (f32[16,32]{1,0:T(8,128)}, f32[16,32]{1,0:T(8,128)S(1)}, u32[]{:S(2)}) copy-start(f32[16,32]{1,0:T(8,128)S(1)} %copy.304) | copy-start | bytes 6148
  196.0 4.3 %copy-start.39 = (s32[2]{0:T(128)S(1)}, s32[2]{0:T(128)}, u32[]{:S(2)}) copy-start(s32[2]{0:T(128)} %copy-done.38) | copy-start | bytes 28
  196.0 4.3 %copy-start.54 = (f32[2,32]{1,0:T(2,128)S(1)}, f32[2,32]{1,0:T(2,128)}, u32[]{:S(2)}) copy-start(f32[2,32]{1,0:T(2,128)} %get-tuple-element.20) | copy-start | bytes 772
  196.0 4.6 %copy-start.53 = (f32[2,32]{1,0:T(2,128)S(1)}, f32[2,32]{1,0:T(2,128)}, u32[]{:S(2)}) copy-start(f32[2,32]{1,0:T(2,128)} %get-tuple-element.19) | copy-start | bytes 772
  196.0 5.0 %copy-start.52 = (f32[2,32]{1,0:T(2,128)S(1)}, f32[2,32]{1,0:T(2,128)}, u32[]{:S(2)}) copy-start(f32[2,32]{1,0:T(2,128)} %get-tuple-element.18) | copy-start | bytes 772
  196.0 5.9 %copy-start.51 = (f32[2,32]{1,0:T(2,128)S(1)}, f32[2,32]{1,0:T(2,128)}, u32[]{:S(2)}) copy-start(f32[2,32]{1,0:T(2,128)} %get-tuple-element.17) | copy-start | bytes 772
  196.0 6.9 %copy-start.50 = (f32[2,32]{1,0:T(2,128)S(1)}, f32[2,32]{1,0:T(2,128)}, u32[]{:S(2)}) copy-start(f32[2,32]{1,0:T(2,128)} %get-tuple-element.16) | copy-start | bytes 772
  196.0 7.8 %copy-start.49 = (f32[2,32]{1,0:T(2,128)S(1)}, f32[2,32]{1,0:T(2,128)}, u32[]{:S(2)}) copy-start(f32[2,32]{1,0:T(2,128)} %get-tuple-element.15) | copy-start | bytes 772
  196.0 8.7 %copy-start.48 = (f32[2,32]{1,0:T(2,128)S(1)}, f32[2,32]{1,0:T(2,128)}, u32[]{:S(2)}) copy-start(f32[2,32]{1,0:T(2,128)} %get-tuple-element.14) | copy-start | bytes 772
  196.0 9.1 %copy-start.47 = (f32[2,32]{1,0:T(2,128)S(1)}, f32[2,32]{1,0:T(2,128)}, u32[]{:S(2)}) copy-start(f32[2,32]{1,0:T(2,128)} %get-tuple-element.13) | copy-start | bytes 772
  200.2 10.2 %copy-start.30 = (f32[2,32,128]{2,1,0:T(8,128)S(1)}, f32[2,32,128]{2,1,0:T(8,128)}, u32[]{:S(2)}) copy-start(f32[2,32,128]{2,1,0:T(8,128)} %fusion.104) | copy-start | bytes 98308
  200.3 10.6 %copy-start.23 = (f32[16,32]{1,0:T(8,128)S(1)}, f32[16,32]{1,0:T(8,128)}, u32[]{:S(2)}) copy-start(f32[16,32]{1,0:T(8,128)} %copy-done.22) | copy-start | bytes 6148
  207.1 7.9 %copy-start.29 = (f32[2,32,128]{2,1,0:T(8,128)S(1)}, f32[2,32,128]{2,1,0:T(8,128)}, u32[]{:S(2)}) copy-start(f32[2,32,128]{2,1,0:T(8,128)} %fusion.106) | copy-start | bytes 98308
  209.4 6.0 %copy-start.21 = (f32[16,32]{1,0:T(8,128)S(1)}, f32[16,32]{1,0:T(8,128)}, u32[]{:S(2)}) copy-start(f32[16,32]{1,0:T(8,128)} %copy-done.20) | copy-start | bytes 6148
  210.9 8.6 %copy-start.28 = (f32[2,32,128]{2,1,0:T(8,128)S(1)}, f32[2,32,128]{2,1,0:T(8,128)}, u32[]{:S(2)}) copy-start(f32[2,32,128]{2,1,0:T(8,128)} %fusion.108) | copy-start | bytes 98308
  213.2 6.7 %copy-start.19 = (f32[16,32]{1,0:T(8,128)S(1)}, f32[16,32]{1,0:T(8,128)}, u32[]{:S(2)}) copy-start(f32[16,32]{1,0:T(8,128)} %copy-done.18) | copy-start | bytes 6148
  215.4 8.6 %copy-start.27 = (f32[2,32,128]{2,1,0:T(8,128)S(1)}, f32[2,32,128]{2,1,0:T(8,128)}, u32[]{:S(2)}) copy-start(f32[2,32,128]{2,1,0:T(8,128)} %fusion.110) | copy-start | bytes 98308
  217.7 6.7 %copy-start.17 = (f32[16,32]{1,0:T(8,128)S(1)}, f32[16,32]{1,0:T(8,128)}, u32[]{:S(2)}) copy-start(f32[16,32]{1,0:T(8,128)} %copy-done.16) | copy-start | bytes 6148
  220.0 8.6 %copy-start.26 = (f32[2,32,128]{2,1,0:T(8,128)S(1)}, f32[2,32,128]{2,1,0:T(8,128)}, u32[]{:S(2)}) copy-start(f32[2,32,128]{2,1,0:T(8,128)} %fusion.112) | copy-start | bytes 98308
  222.3 6.7 %copy-start.15 = (f32[16,32]{1,0:T(8,128)S(1)}, f32[16,32]{1,0:T(8,128)}, u32[]{:S(2)}) copy-start(f32[16,32]{1,0:T(8,128)} %copy-done.14) | copy-start | bytes 6148
  224.5 8.2 %copy-start.25 = (f32[2,32,128]{2,1,0:T(8,128)S(1)}, f32[2,32,128]{2,1,0:T(8,128)}, u32[]{:S(2)}) copy-start(f32[2,32,128]{2,1,0:T(8,128)} %fusion.114) | copy-start | bytes 98308
  229.0 6.2 %copy-start.24 = (f32[2,32,128]{2,1,0:T(8,128)S(1)}, f32[2,32,128]{2,1,0:T(8,128)}, u32[]{:S(2)}) copy-start(f32[2,32,128]{2,1,0:T(8,128)} %fusion.116) | copy-start | bytes 98308
  235.2 5.5 %copy-start.6 = (f32[16,4,1024]{2,1,0:T(4,128)S(1)}, f32[16,4,1024]{2,1,0:T(4,128)}, u32[]{:S(2)}) copy-start(f32[16,4,1024]{2,1,0:T(4,128)} %reshape.507) | copy-start | bytes 786436
  235.6 5.1 %copy-start.5 = (f32[16,4,1024]{2,1,0:T(4,128)S(1)}, f32[16,4,1024]{2,1,0:T(4,128)}, u32[]{:S(2)}) copy-start(f32[16,4,1024]{2,1,0:T(4,128)} %reshape.508) | copy-start | bytes 786436
  235.6 5.3 %copy-start.4 = (f32[16,4,1024]{2,1,0:T(4,128)S(1)}, f32[16,4,1024]{2,1,0:T(4,128)}, u32[]{:S(2)}) copy-start(f32[16,4,1024]{2,1,0:T(4,128)} %reshape.509) | copy-start | bytes 786436
  237.0 4.0 %copy-start.3 = (f32[16,4,1024]{2,1,0:T(4,128)S(1)}, f32[16,4,1024]{2,1,0:T(4,128)}, u32[]{:S(2)}) copy-start(f32[16,4,1024]{2,1,0:T(4,128)} %reshape.510) | copy-start | bytes 786436
  240.9 59.6 %copy-start.42 = (f32[1,4,64]{2,1,0:T(4,128)S(1)}, f32[1,4,64]{2,1,0:T(4,128)}, u32[]{:S(2)}) copy-start(f32[1,4,64]{2,1,0:T(4,128)} %copy-done.41) | copy-start | bytes 3076
  240.9 59.6 %copy-start.44 = (f32[1,4,64]{2,1,0:T(4,128)S(1)}, f32[1,4,64]{2,1,0:T(4,128)}, u32[]{:S(2)}) copy-start(f32[1,4,64]{2,1,0:T(4,128)} %reshape.527) | copy-start | bytes 3076
  240.9 59.6 %copy-start.45 = (f32[1,4,64]{2,1,0:T(4,128)S(1)}, f32[1,4,64]{2,1,0:T(4,128)}, u32[]{:S(2)}) copy-start(f32[1,4,64]{2,1,0:T(4,128)} %reshape.528) | copy-start | bytes 3076
  240.9 98.4 %copy-start.43 = (f32[4,64]{1,0:T(4,128)S(1)}, f32[4,64]{1,0:T(4,128)}, u32[]{:S(2)}) copy-start(f32[4,64]{1,0:T(4,128)} %get-tuple-element.29) | copy-start | bytes 3076
  241.0 98.5 %copy-start.7 = (f32[1,4,8,8,128]{4,3,2,0,1:T(8,128)S(1)}, f32[1,4,8,8,128]{4,3,2,0,1:T(8,128)}, u32[]{:S(2)}) copy-start(f32[1,4,8,8,128]{4,3,2,0,1:T(8,128)} %copy.339) | copy-start | bytes 393220
  (9 other events, 12.7 us)
Sparse Core Ops, SparseCore 0:
  9.5 40.6 all-gather.1
  242.5 95.1 all-reduce.3
where the time goes:
time: 350 us; the launch traced here: 347 us
  blocking collectives  118 us (34%)
  waiting for transfers between devices  71.5 us (20%)
  local copies, waits for them, and re-layouts  68.2 us (19%)
  matrix products  56.5 us (16%)
  other arithmetic  19.1 us (5%)
  between operations  14.3 us (4%)
    pmax x1, blocking collectives, body(): lax.pmax(nearby_maximum.astype(jnp.bfloat16), 'seq')  59.7 us
    unnamed x1, blocking collectives  57.9 us
    unnamed x3, waiting for transfers between devices  37.2 us
    all_gather x1, waiting for transfers between devices, body(): gathered = lax.all_gather(queries, 'seq', axis=0, tiled=True)  34.3 us
    dot_general x8, matrix products, accumulate(): jnp.einsum('lip,pn->lin', prefix_weights.astype(jnp.bfloat16), head_colum...  16.1 us
    dot_general x8, matrix products, score_blocks(): jnp.einsum('rux,zx->ruz', row_queries, head_column_span(base_cache, head_...  15.1 us
    dot_general x8, matrix products, accumulate(): jnp.einsum('pqk,pkd->pqd', page_weights.astype(jnp.bfloat16), head_column...  12.6 us
    reshape x8, local copies, waits for them, and re-layouts, accumulate(): numerator.reshape(overall_rows, step_count, group_size * HD)  11.4 us
  transfers between devices with their start and end apart: 2, of which 2 were waited for; matrix products, arithmetic and copies ran while one was open for 3% of the time, Pallas kernels for 0%

commit v1 on v0

v1 whole, which is shorter than its diff:
```python
import functools
import math

import jax
import jax.numpy as jnp
from jax import lax
from jax.experimental import pallas as pl
from jax.experimental.pallas import tpu as pltpu
from jax.sharding import PartitionSpec as P

QH = 64
KVH = 8
HD = 128
GROUP = QH // KVH
CHUNKS = 4
HC = KVH // CHUNKS
FAR = -1e30
COEF = HD**-0.5 * math.log2(math.e)


def kernel(
    n,
    table_ref,
    offsets_ref,
    lengths_ref,
    q_ref,
    new_ref,
    base_hbm,
    pool_hbm,
    out_ref,
    kv,
    limits,
    spread,
    gathered,
    part,
    part_ml,
    core_in,
    core_in_ml,
    yhalf,
    yhalf_ml,
    y_in,
    y_in_ml,
    zsend,
    zsend_ml,
    z_in,
    z_in_ml,
    factors,
    load_sem,
    gz_send,
    gz_recv,
    gy_send,
    gy_recv,
    gc_send,
    gc_recv,
    rc_send,
    rc_recv,
    ry_send,
    ry_recv,
    rz_send,
    rz_recv,
):
    steps = q_ref.shape[1]
    block = GROUP * steps
    planes = n // 4
    quarter = planes * block
    lanes = n * block
    base_len = base_hbm.shape[0]
    pages_here, page_len, _ = pool_hbm.shape
    rows, slots = table_ref.shape
    pages_at = base_len
    new_at = base_len + pages_here * page_len
    new_pad = kv.shape[0] - new_at

    me = lax.axis_index("seq")
    core = lax.rem(me, 2)
    y = lax.rem(lax.div(me, 2), 2)
    plane = lax.div(me, 4)
    position = core * (2 * planes) + y * planes + plane
    core_peer = plane * 4 + y * 2 + (1 - core)
    y_peer = plane * 4 + (1 - y) * 2 + core

    def plane_at(j):
        return lax.rem(plane + j, planes)

    def plane_before(j):
        return lax.rem(plane + planes - j, planes)

    def z_peer(j):
        return plane_at(j) * 4 + y * 2 + core

    loads = [pltpu.make_async_copy(base_hbm, kv.at[pl.ds(0, base_len)], load_sem.at[0])]
    for p in range(pages_here):
        loads.append(
            pltpu.make_async_copy(
                pool_hbm.at[p],
                kv.at[pl.ds(pages_at + p * page_len, page_len)],
                load_sem.at[1 + p],
            )
        )
    for load in loads:
        load.start()

    barrier = pltpu.get_barrier_semaphore()
    peers = [core_peer, y_peer] + [z_peer(j) for j in range(1, planes)]
    for peer in peers:
        pl.semaphore_signal(
            barrier, inc=1, device_id={"seq": peer}, device_id_type=pl.DeviceIdType.MESH
        )

    wide = q_ref[0].astype(jnp.float32)
    for i in range(QH):
        spread[i * steps : (i + 1) * steps, :] = wide[:, i * HD : (i + 1) * HD]
    own = spread[...].astype(jnp.bfloat16)
    own_at = pl.multiple_of(position * block, block)
    for h in range(KVH):
        gathered[h, pl.ds(own_at, block), :] = own[h * block : (h + 1) * block, :]

    pl.semaphore_wait(barrier, len(peers))

    def remote(src, dst, send, recv, peer):
        return pltpu.make_async_remote_copy(
            src_ref=src,
            dst_ref=dst,
            send_sem=send,
            recv_sem=recv,
            device_id={"seq": peer},
            device_id_type=pl.DeviceIdType.MESH,
        )

    def rows_of(c, first, count):
        return gathered.at[
            pl.ds(c * HC, HC), pl.ds(pl.multiple_of(first * block, block), count * block)
        ]

    def gather_z(c, j):
        ref = rows_of(c, position, 1)
        return remote(ref, ref, gz_send.at[c, j - 1], gz_recv.at[c, j - 1], z_peer(j))

    def gather_z_in(c, j):
        ref = rows_of(c, core * (2 * planes) + y * planes + plane_before(j), 1)
        return remote(ref, ref, gz_send.at[c, j - 1], gz_recv.at[c, j - 1], z_peer(j))

    def gather_y(c):
        ref = rows_of(c, core * (2 * planes) + y * planes, planes)
        return remote(ref, ref, gy_send.at[c], gy_recv.at[c], y_peer)

    def gather_y_in(c):
        ref = rows_of(c, core * (2 * planes) + (1 - y) * planes, planes)
        return remote(ref, ref, gy_send.at[c], gy_recv.at[c], y_peer)

    def gather_core(c, which):
        yy = y if which == 0 else 1 - y
        ref = rows_of(c, core * (2 * planes) + yy * planes, planes)
        return remote(ref, ref, gc_send.at[c, which], gc_recv.at[c, which], core_peer)

    def gather_core_in(c, which):
        yy = y if which == 0 else 1 - y
        ref = rows_of(c, (1 - core) * (2 * planes) + yy * planes, planes)
        return remote(ref, ref, gc_send.at[c, which], gc_recv.at[c, which], core_peer)

    def core_copies(c):
        theirs = pl.ds((1 - core) * 2, 2)
        return (
            remote(part.at[c, theirs], core_in.at[c], rc_send.at[c, 0], rc_recv.at[c, 0], core_peer),
            remote(
                part_ml.at[c, theirs], core_in_ml.at[c], rc_send.at[c, 1], rc_recv.at[c, 1], core_peer
            ),
        )

    def y_copies(c):
        return (
            remote(yhalf.at[c, 1 - y], y_in.at[c], ry_send.at[c, 0], ry_recv.at[c, 0], y_peer),
            remote(yhalf_ml.at[c, 1 - y], y_in_ml.at[c], ry_send.at[c, 1], ry_recv.at[c, 1], y_peer),
        )

    def z_copies(c, j):
        theirs = pl.ds(pl.multiple_of(plane_at(j) * block, block), block)
        return (
            remote(
                zsend.at[c, :, theirs],
                z_in.at[c, j - 1],
                rz_send.at[c, j - 1, 0],
                rz_recv.at[c, j - 1, 0],
                z_peer(j),
            ),
            remote(
                zsend_ml.at[c],
                z_in_ml.at[c, j - 1],
                rz_send.at[c, j - 1, 1],
                rz_recv.at[c, j - 1, 1],
                z_peer(j),
            ),
        )

    for c in range(CHUNKS):
        for j in range(1, planes):
            gather_z(c, j).start()

    lane = lax.broadcasted_iota(jnp.int32, (1, lanes), 1)
    lane_block = lax.div(lane, block)
    base_limit = jnp.zeros((1, lanes), jnp.int32)
    page_limits = [jnp.zeros((1, lanes), jnp.int32) for _ in range(pages_here)]
    for b in range(rows):
        at = (b % 2) * (2 * planes) + (b // 2 % 2) * planes + b // 4
        here = lane_block == at
        base_limit = jnp.where(here, offsets_ref[b] - me * base_len, base_limit)
        for p in range(pages_here):
            live = jnp.int32(0)
            for s in range(slots):
                live = live + jnp.where(
                    table_ref[b, s] == me * pages_here + p, lengths_ref[b] - s * page_len, 0
                )
            page_limits[p] = jnp.where(here, live, page_limits[p])
    new_limit = jnp.where(lane_block == position, lax.rem(lane, steps) + 1, 0)
    for i, limit in enumerate([base_limit] + page_limits + [new_limit]):
        limits[i : i + 1, :] = limit
    kv[new_at:, :] = jnp.concatenate(
        [new_ref[0].astype(jnp.float32), jnp.zeros((new_pad - steps, kv.shape[1]), jnp.float32)],
        axis=0,
    ).astype(jnp.bfloat16)

    key_blocks = [(0, base_len)]
    key_blocks += [(pages_at + p * page_len, page_len) for p in range(pages_here)]
    key_blocks += [(new_at, new_pad)]
    width = min(lanes, 512)
    per_width = width // quarter

    def forward_first(c):
        for j in range(1, planes):
            gather_z_in(c, j).wait_recv()
        gather_y(c).start()
        gather_core(c, 0).start()

    def forward_second(c):
        gather_y_in(c).wait_recv()
        gather_core(c, 1).start()

    def attend(c):
        gather_core_in(c, 0).wait_recv()
        gather_core_in(c, 1).wait_recv()

        def lane_part(lb):
            start = pl.multiple_of(lb * width, width)
            tops, totals = [], []
            for hh in range(HC):
                h = c * HC + hh
                queries = gathered[h, pl.ds(start, width), :]
                keys = kv[:, 2 * h * HD : (2 * h + 1) * HD]
                values = kv[:, (2 * h + 1) * HD : (2 * h + 2) * HD]
                scores = lax.dot_general(
                    keys, queries, (((1,), (1,)), ((), ())), preferred_element_type=jnp.float32
                )
                pieces = []
                for i, (at, count) in enumerate(key_blocks):
                    key = lax.broadcasted_iota(jnp.int32, (count, width), 0)
                    limit = limits[i : i + 1, pl.ds(start, width)]
                    pieces.append(jnp.where(key < limit, scores[at : at + count], FAR))
                top = functools.reduce(
                    jnp.maximum, [jnp.max(x, axis=0, keepdims=True) for x in pieces]
                )
                weights = [jnp.exp2((x - top) * COEF) for x in pieces]
                total = sum(jnp.sum(x, axis=0, keepdims=True) for x in weights)
                rounded = jnp.concatenate([x.astype(jnp.bfloat16) for x in weights], axis=0)
                sums = lax.dot_general(
                    values, rounded, (((0,), (0,)), ((), ())), preferred_element_type=jnp.float32
                ).astype(jnp.bfloat16)
                for i in range(per_width):
                    part[c, lb * per_width + i, hh] = sums[:, i * quarter : (i + 1) * quarter]
                tops.append(top)
                totals.append(total)
            pad = [jnp.zeros((4 - HC, width), jnp.float32)] if HC < 4 else []
            both = jnp.concatenate(tops + pad + totals + pad, axis=0)
            for i in range(per_width):
                part_ml[c, lb * per_width + i] = both[:, i * quarter : (i + 1) * quarter]

        if lanes == width:
            lane_part(0)
        else:
            lax.fori_loop(0, lanes // width, lambda lb, _: (lane_part(lb), 0)[1], 0)
        for copy in core_copies(c):
            copy.start()

    def merge_ml(mine, theirs):
        top = jnp.maximum(mine[:4], theirs[:4])
        a = jnp.exp2((mine[:4] - top) * COEF)
        b = jnp.exp2((theirs[:4] - top) * COEF)
        return a, b, jnp.concatenate([top, a * mine[4:] + b * theirs[4:]], axis=0)

    def merge_core(c):
        for copy in core_copies(c):
            copy.wait_recv()
        for yy in range(2):
            a, b, ml = merge_ml(part_ml[c, core * 2 + yy], core_in_ml[c, yy])
            yhalf_ml[c, yy] = ml
            for hh in range(HC):
                merged = part[c, core * 2 + yy, hh].astype(jnp.float32) * a[hh : hh + 1]
                merged = merged + core_in[c, yy, hh].astype(jnp.float32) * b[hh : hh + 1]
                yhalf[c, yy, hh] = merged.astype(jnp.bfloat16)
        for copy in y_copies(c):
            copy.start()

    def merge_y(c):
        for copy in y_copies(c):
            copy.wait_recv()
        a, b, ml = merge_ml(yhalf_ml[c, y], y_in_ml[c])
        zsend_ml[c] = ml
        for hh in range(HC):
            merged = yhalf[c, y, hh].astype(jnp.float32) * a[hh : hh + 1]
            merged = merged + y_in[c, hh].astype(jnp.float32) * b[hh : hh + 1]
            zsend[c, hh] = merged.T.astype(jnp.bfloat16)
        for j in range(1, planes):
            for copy in z_copies(c, j):
                copy.start()

    def finish(c):
        for j in range(1, planes):
            for copy in z_copies(c, j):
                copy.wait_recv()
        parts = [zsend_ml[c]] + [z_in_ml[c, j - 1] for j in range(1, planes)]
        top = functools.reduce(jnp.maximum, [x[:4] for x in parts])
        scales = [jnp.exp2((x[:4] - top) * COEF) for x in parts]
        total = sum(s * x[4:] for s, x in zip(scales, parts))
        scales = [s / total if HC == 4 else s[:HC] / total[:HC] for s in scales]
        pad = [jnp.zeros((HD - planes * HC, quarter), jnp.float32)]
        factors[c] = jnp.concatenate(scales + pad, axis=0).T
        mine = pl.ds(pl.multiple_of(plane * block, block), block)
        by_source = factors[c, mine, :]
        for hh in range(HC):
            h = c * HC + hh
            result = zsend[c, hh, mine, :].astype(jnp.float32) * by_source[:, hh : hh + 1]
            for j in range(1, planes):
                at = j * HC + hh
                result = result + z_in[c, j - 1, hh].astype(jnp.float32) * by_source[:, at : at + 1]
            for g in range(GROUP):
                at = (h * GROUP + g) * HD
                out_ref[0, :, at : at + HD] = result[g * steps : (g + 1) * steps, :].astype(
                    jnp.bfloat16
                )

    for t in range(CHUNKS + 5):
        if 0 <= t < CHUNKS:
            forward_first(t)
        if 0 <= t - 1 < CHUNKS:
            forward_second(t - 1)
        if t == 2:
            for load in loads:
                load.wait()
        if 0 <= t - 2 < CHUNKS:
            attend(t - 2)
        if 0 <= t - 3 < CHUNKS:
            merge_core(t - 3)
        if 0 <= t - 4 < CHUNKS:
            merge_y(t - 4)
        if 0 <= t - 5 < CHUNKS:
            finish(t - 5)

    for c in range(CHUNKS):
        for j in range(1, planes):
            gather_z(c, j).wait_send()
            for copy in z_copies(c, j):
                copy.wait_send()
        gather_y(c).wait_send()
        gather_core(c, 0).wait_send()
        gather_core(c, 1).wait_send()
        for copy in core_copies(c) + y_copies(c):
            copy.wait_send()


def body(n, queries, base_cache, page_pool, new_cache, page_table, offsets, lengths):
    steps = queries.shape[1]
    block = GROUP * steps
    planes = n // 4
    quarter = planes * block
    lanes = n * block
    pages_here, page_len, columns = page_pool.shape
    keys = base_cache.shape[0] + pages_here * page_len + 16
    bf16, f32 = jnp.bfloat16, jnp.float32
    dma = pltpu.SemaphoreType.DMA
    smem = pl.BlockSpec(memory_space=pltpu.SMEM)
    vmem = pl.BlockSpec(memory_space=pltpu.VMEM)
    hbm = pl.BlockSpec(memory_space=pl.ANY)
    return pl.pallas_call(
        functools.partial(kernel, n),
        out_shape=jax.ShapeDtypeStruct(queries.shape, bf16),
        in_specs=[smem, smem, smem, vmem, vmem, hbm, hbm],
        out_specs=vmem,
        scratch_shapes=[
            pltpu.VMEM((keys, columns), bf16),
            pltpu.VMEM((max(8, pages_here + 2), lanes), jnp.int32),
            pltpu.VMEM((QH * steps, HD), f32),
            pltpu.VMEM((KVH, lanes, HD), bf16),
            pltpu.VMEM((CHUNKS, 4, HC, HD, quarter), bf16),
            pltpu.VMEM((CHUNKS, 4, 8, quarter), f32),
            pltpu.VMEM((CHUNKS, 2, HC, HD, quarter), bf16),
            pltpu.VMEM((CHUNKS, 2, 8, quarter), f32),
            pltpu.VMEM((CHUNKS, 2, HC, HD, quarter), bf16),
            pltpu.VMEM((CHUNKS, 2, 8, quarter), f32),
            pltpu.VMEM((CHUNKS, HC, HD, quarter), bf16),
            pltpu.VMEM((CHUNKS, 8, quarter), f32),
            pltpu.VMEM((CHUNKS, HC, quarter, HD), bf16),
            pltpu.VMEM((CHUNKS, 8, quarter), f32),
            pltpu.VMEM((CHUNKS, planes - 1, HC, block, HD), bf16),
            pltpu.VMEM((CHUNKS, planes - 1, 8, quarter), f32),
            pltpu.VMEM((CHUNKS, quarter, HD), f32),
            dma((1 + pages_here,)),
            dma((CHUNKS, planes - 1)),
            dma((CHUNKS, planes - 1)),
            dma((CHUNKS,)),
            dma((CHUNKS,)),
            dma((CHUNKS, 2)),
            dma((CHUNKS, 2)),
            dma((CHUNKS, 2)),
            dma((CHUNKS, 2)),
            dma((CHUNKS, 2)),
            dma((CHUNKS, 2)),
            dma((CHUNKS, planes - 1, 2)),
            dma((CHUNKS, planes - 1, 2)),
        ],
        compiler_params=pltpu.CompilerParams(
            collective_id=0, has_side_effects=True, vmem_limit_bytes=56 * 1024 * 1024
        ),
    )(page_table, offsets, lengths, queries, new_cache, base_cache, page_pool)


def solution(mesh):
    in_specs = (
        P(("groups", "seq"), None, None),
        P(("groups", "seq"), None),
        P(("groups", "seq"), None, None),
        P(("groups", "seq"), None, None),
        P("groups", None),
        P("groups"),
        P("groups"),
    )
    return jax.shard_map(
        functools.partial(body, mesh.shape["seq"]),
        mesh=mesh,
        in_specs=in_specs,
        out_specs=P(("groups", "seq"), None, None),
        check_vma=False,
    )
```

time: 350 us -> 39.9 us (0.11)
  blocking collectives: 118 us -> 0 us
  waiting for transfers between devices: 71.5 us -> 0 us
  local copies, waits for them, and re-layouts: 68.2 us -> 2.85 us
  matrix products: 56.5 us -> 0 us
  Pallas kernels: 0 us -> 36.8 us
  other arithmetic: 19.1 us -> 0 us
  between operations: 14.3 us -> 0.01 us
    pmax x1 -> x0, blocking collectives: 59.7 us -> none  [body(): lax.pmax(nearby_maximum.astype(jnp.bfloat16), 'seq')]
    unnamed x1 -> x0, blocking collectives: 57.9 us -> none
    dot_general x50 -> x0, matrix products: 56.5 us -> none  [the longest x8 16.1 us: accumulate(): jnp.einsum('lip,pn->lin', prefix_weights.astype(jnp.bfloat16), head_colum...]
    unnamed x3 -> x0, waiting for transfers between devices: 37.2 us -> none
    pallas_call x0 -> x1, Pallas kernels: none -> 36.8 us  [body(): pl.pallas_call(functools.partial(kernel, n), out_shape=jax.ShapeDtypeStru...]
    all_gather x1 -> x0, waiting for transfers between devices: 34.3 us -> none  [body(): gathered = lax.all_gather(queries, 'seq', axis=0, tiled=True)]
    reshape x28 -> x0, local copies, waits for them, and re-layouts: 17.3 us -> none  [the longest x8 11.4 us: accumulate(): numerator.reshape(overall_rows, step_count, group_size * HD)]
    gather x10 -> x0, local copies, waits for them, and re-layouts: 11.9 us -> none  [the longest x8 9.38 us: accumulate(): page_top = row_top[owner_row]]
  transfers between devices with their start and end apart: 2 -> 0, of which waited for: 2 -> 0; matrix products, arithmetic and copies ran while one was open for 3% -> 0% of each run, Pallas kernels for 0% -> 0%
where the time goes in v1:
time: 39.9 us; the launch traced here: 39.7 us
  Pallas kernels  36.8 us (92%)
  local copies, waits for them, and re-layouts  2.85 us (7%)
    pallas_call x1, Pallas kernels, body(): pl.pallas_call(functools.partial(kernel, n), out_shape=jax.ShapeDtypeStru...  36.8 us
    unnamed x2, local copies, waits for them, and re-layouts  2.85 us

profile of v1, /device:TPU:0, one launch (start us, length us, event | category | flops | bytes accessed | tf_op | source)
XLA Modules:
  0.0 39.7 jit_solution(2014957136314500130)
XLA Ops:
  0.0 1.4 %copy.8.table_ref = s32[16,2]{1,0:T(8,128)} copy(s32[16,2]{0,1:T(2,128)} %param.11) | data formatting | bytes 256 | tf_op args[4]
  1.4 36.8 %shard_map.73 = bf16[1,4,8192]{2,1,0:T(4,128)(2,1)} custom-call(s32[16,2]{1,0:T(8,128)} %copy.8.table_ref, s32[16]{0:T(128)} %offsets_ref.1, s32[16]{0:T(128)} %lengths_ref.1, bf16[1,4,8192]{2,1,0:T(4,128)(2,1)} %q_ref.1, bf16[1,4,2048]{2,1,0:T(4,128)(2,1)} %new_ref.1, bf16[512,2048]{1,0:T(8,128)(2,1)} %base_hbm.1, bf16[2,128,2048]{2,1,0:T(8,128)(2,1)} %pool_hbm.1), custom_call_target="tpu_custom_call" | custom-call | tf_op jit(solution)/shard_map/pallas_call | solution.py:382
  38.2 1.5 %copy.10 = bf16[1,4,8192]{2,1,0:T(4,128)(2,1)} copy(bf16[1,4,8192]{2,1,0:T(4,128)(2,1)} %shard_map.73) | data formatting | bytes 131072

commit v2 on v1

--- a/solution.py
+++ b/solution.py
@@ -14,6 +14,32 @@
 GROUP = QH // KVH
 CHUNKS = 4
 HC = KVH // CHUNKS
+SCHEDULE = [
+    ("gather z", 0),
+    ("gather z", 1),
+    ("gather y", 0),
+    ("gather z", 2),
+    ("gather y", 1),
+    ("attend", 0),
+    ("gather z", 3),
+    ("gather y", 2),
+    ("attend", 1),
+    ("core", 0),
+    ("gather y", 3),
+    ("attend", 2),
+    ("core", 1),
+    ("y", 0),
+    ("attend", 3),
+    ("core", 2),
+    ("y", 1),
+    ("core", 3),
+    ("y", 2),
+    ("z", 0),
+    ("y", 3),
+    ("z", 1),
+    ("z", 2),
+    ("z", 3),
+]
 FAR = -1e30
 COEF = HD**-0.5 * math.log2(math.e)
 
@@ -66,7 +92,7 @@
     lanes = n * block
     base_len = base_hbm.shape[0]
     pages_here, page_len, _ = pool_hbm.shape
-    rows, slots = table_ref.shape
+    slots, rows = table_ref.shape
     pages_at = base_len
     new_at = base_len + pages_here * page_len
     new_pad = kv.shape[0] - new_at
@@ -192,7 +218,7 @@
             ),
         )
 
-    for c in range(CHUNKS):
+    for c in range(2):
         for j in range(1, planes):
             gather_z(c, j).start()
 
@@ -208,7 +234,7 @@
             live = jnp.int32(0)
             for s in range(slots):
                 live = live + jnp.where(
-                    table_ref[b, s] == me * pages_here + p, lengths_ref[b] - s * page_len, 0
+                    table_ref[s, b] == me * pages_here + p, lengths_ref[b] - s * page_len, 0
                 )
             page_limits[p] = jnp.where(here, live, page_limits[p])
     new_limit = jnp.where(lane_block == position, lax.rem(lane, steps) + 1, 0)
@@ -228,6 +254,8 @@
     def forward_first(c):
         for j in range(1, planes):
             gather_z_in(c, j).wait_recv()
+            if c + 2 < CHUNKS:
+                gather_z(c + 2, j).start()
         gather_y(c).start()
         gather_core(c, 0).start()
 
@@ -337,22 +365,21 @@
                     jnp.bfloat16
                 )
 
-    for t in range(CHUNKS + 5):
-        if 0 <= t < CHUNKS:
-            forward_first(t)
-        if 0 <= t - 1 < CHUNKS:
-            forward_second(t - 1)
-        if t == 2:
+    stages = {
+        "gather z": forward_first,
+        "gather y": forward_second,
+        "attend": attend,
+        "core": merge_core,
+        "y": merge_y,
+        "z": finish,
+    }
+    loaded = False
+    for stage, c in SCHEDULE:
+        if stage == "attend" and not loaded:
+            loaded = True
             for load in loads:
                 load.wait()
-        if 0 <= t - 2 < CHUNKS:
-            attend(t - 2)
-        if 0 <= t - 3 < CHUNKS:
-            merge_core(t - 3)
-        if 0 <= t - 4 < CHUNKS:
-            merge_y(t - 4)
-        if 0 <= t - 5 < CHUNKS:
-            finish(t - 5)
+        stages[stage](c)
 
     for c in range(CHUNKS):
         for j in range(1, planes):
@@ -419,7 +446,7 @@
         compiler_params=pltpu.CompilerParams(
             collective_id=0, has_side_effects=True, vmem_limit_bytes=56 * 1024 * 1024
         ),
-    )(page_table, offsets, lengths, queries, new_cache, base_cache, page_pool)
+    )(page_table.T, offsets, lengths, queries, new_cache, base_cache, page_pool)
 
 
 def solution(mesh):

time: 39.9 us -> 37.1 us (0.930)
  Pallas kernels: 36.8 us -> 35.4 us
  local copies, waits for them, and re-layouts: 2.85 us -> 1.49 us
    pallas_call x1, Pallas kernels: 36.8 us -> 35.4 us  [body(): pl.pallas_call(functools.partial(kernel, n), out_shape=jax.ShapeDtypeStru...]
    unnamed x2 -> x1, local copies, waits for them, and re-layouts: 2.85 us -> 1.49 us
where the time goes in v2:
time: 37.1 us; the launch traced here: 36.9 us
  Pallas kernels  35.4 us (95%)
  local copies, waits for them, and re-layouts  1.49 us (4%)
    pallas_call x1, Pallas kernels, body(): pl.pallas_call(functools.partial(kernel, n), out_shape=jax.ShapeDtypeStru...  35.4 us
    unnamed x1, local copies, waits for them, and re-layouts  1.49 us

profile of v2, /device:TPU:0, one launch (start us, length us, event | category | flops | bytes accessed | tf_op | source)
XLA Modules:
  0.0 36.9 jit_solution(11220194826221714501)
XLA Ops:
  0.0 35.4 %shard_map.73 = bf16[1,4,8192]{2,1,0:T(4,128)(2,1)} custom-call(s32[2,16]{1,0:T(2,128)} %bitcast.1, s32[16]{0:T(128)} %offsets_ref.1, s32[16]{0:T(128)} %lengths_ref.1, bf16[1,4,8192]{2,1,0:T(4,128)(2,1)} %q_ref.1, bf16[1,4,2048]{2,1,0:T(4,128)(2,1)} %new_ref.1, bf16[512,2048]{1,0:T(8,128)(2,1)} %base_hbm.1, bf16[2,128,2048]{2,1,0:T(8,128)(2,1)} %pool_hbm.1), custom_call_target="tpu_custom_call" | custom-call | tf_op jit(solution)/shard_map/pallas_call | solution.py:409
  35.4 1.5 %copy.9 = bf16[1,4,8192]{2,1,0:T(4,128)(2,1)} copy(bf16[1,4,8192]{2,1,0:T(4,128)(2,1)} %shard_map.73) | data formatting | bytes 131072

commit v3 on v2

--- a/solution.py
+++ b/solution.py
@@ -166,13 +166,13 @@
         ref = rows_of(c, core * (2 * planes) + y * planes + plane_before(j), 1)
         return remote(ref, ref, gz_send.at[c, j - 1], gz_recv.at[c, j - 1], z_peer(j))
 
-    def gather_y(c):
-        ref = rows_of(c, core * (2 * planes) + y * planes, planes)
-        return remote(ref, ref, gy_send.at[c], gy_recv.at[c], y_peer)
-
-    def gather_y_in(c):
-        ref = rows_of(c, core * (2 * planes) + (1 - y) * planes, planes)
-        return remote(ref, ref, gy_send.at[c], gy_recv.at[c], y_peer)
+    def gather_y(c, k):
+        ref = rows_of(c, core * (2 * planes) + y * planes + plane_before(k), 1)
+        return remote(ref, ref, gy_send.at[c, k], gy_recv.at[c, k], y_peer)
+
+    def gather_y_in(c, k):
+        ref = rows_of(c, core * (2 * planes) + (1 - y) * planes + plane_before(k), 1)
+        return remote(ref, ref, gy_send.at[c, k], gy_recv.at[c, k], y_peer)
 
     def gather_core(c, which):
         yy = y if which == 0 else 1 - y
@@ -219,6 +219,7 @@
         )
 
     for c in range(2):
+        gather_y(c, 0).start()
         for j in range(1, planes):
             gather_z(c, j).start()
 
@@ -254,13 +255,16 @@
     def forward_first(c):
         for j in range(1, planes):
             gather_z_in(c, j).wait_recv()
+            gather_y(c, j).start()
             if c + 2 < CHUNKS:
                 gather_z(c + 2, j).start()
-        gather_y(c).start()
+        if c + 2 < CHUNKS:
+            gather_y(c + 2, 0).start()
         gather_core(c, 0).start()
 
     def forward_second(c):
-        gather_y_in(c).wait_recv()
+        for k in range(planes):
+            gather_y_in(c, k).wait_recv()
         gather_core(c, 1).start()
 
     def attend(c):
@@ -386,7 +390,8 @@
             gather_z(c, j).wait_send()
             for copy in z_copies(c, j):
                 copy.wait_send()
-        gather_y(c).wait_send()
+        for k in range(planes):
+            gather_y(c, k).wait_send()
         gather_core(c, 0).wait_send()
         gather_core(c, 1).wait_send()
         for copy in core_copies(c) + y_copies(c):
@@ -432,8 +437,8 @@
             dma((1 + pages_here,)),
             dma((CHUNKS, planes - 1)),
             dma((CHUNKS, planes - 1)),
-            dma((CHUNKS,)),
-            dma((CHUNKS,)),
+            dma((CHUNKS, planes)),
+            dma((CHUNKS, planes)),
             dma((CHUNKS, 2)),
             dma((CHUNKS, 2)),
             dma((CHUNKS, 2)),

time: 37.1 us -> 36.7 us (0.989)
  Pallas kernels: 35.4 us -> 35 us
where the time goes in v3:
time: 36.7 us; the launch traced here: 36.5 us
  Pallas kernels  35 us (95%)
  local copies, waits for them, and re-layouts  1.49 us (4%)
    pallas_call x1, Pallas kernels, body(): pl.pallas_call(functools.partial(kernel, n), out_shape=jax.ShapeDtypeStru...  35 us
    unnamed x1, local copies, waits for them, and re-layouts  1.49 us

profile of v3, /device:TPU:0, one launch (start us, length us, event | category | flops | bytes accessed | tf_op | source)
XLA Modules:
  0.0 36.5 jit_solution(264222831104885663)
XLA Ops:
  0.0 35.0 %shard_map.73 = bf16[1,4,8192]{2,1,0:T(4,128)(2,1)} custom-call(s32[2,16]{1,0:T(2,128)} %bitcast.1, s32[16]{0:T(128)} %offsets_ref.1, s32[16]{0:T(128)} %lengths_ref.1, bf16[1,4,8192]{2,1,0:T(4,128)(2,1)} %q_ref.1, bf16[1,4,2048]{2,1,0:T(4,128)(2,1)} %new_ref.1, bf16[512,2048]{1,0:T(8,128)(2,1)} %base_hbm.1, bf16[2,128,2048]{2,1,0:T(8,128)(2,1)} %pool_hbm.1), custom_call_target="tpu_custom_call" | custom-call | tf_op jit(solution)/shard_map/pallas_call | solution.py:414
  35.0 1.5 %copy.9 = bf16[1,4,8192]{2,1,0:T(4,128)(2,1)} copy(bf16[1,4,8192]{2,1,0:T(4,128)(2,1)} %shard_map.73) | data formatting | bytes 131072
